TPU v7x, 256 devices: a whole 4x4x8 slice. The times are simulated.
256 devices in a mesh: branch: 8 (over y, core), slot: 32 (over x, z).
Axes of the slice: x: 4, y: 4, z: 8, core: 2. Of those that a mesh axis runs over, the one named last changes fastest.
Arguments:
- kkt_inverse: bfloat16 [2048, 2048], replicated
- cost: float32 [16384, 2048], P(('branch', 'slot'))
- anchor: float32 [16384, 2048], P(('branch', 'slot')), may hold values from 0 to 2
- capacity: float32 [16384, 2048], P(('branch', 'slot')), may hold values from 0.5 to 3
- multiplier: float32 [16384, 1536], P(('branch', 'slot')), may hold values from -3 to 3
- penalty: float32 [2048], replicated, may hold values from 0.5 to 2
- weight: int32 [16384], P(('branch', 'slot')), may hold values from 1 to 16
- node_two: int32 [16384], P(('branch', 'slot')), may hold values from 0 to 255, as said below
- node_three: int32 [16384], P(('branch', 'slot')), may hold values from 0 to 1023, as said below
Outputs:
- solution: float32 [16384, 2048], P(('branch', 'slot'))
- new_multiplier: float32 [16384, 1536], P(('branch', 'slot'))
Inputs may be any that keep to these rules, and one draw needn't show every extreme that they name: `node_three`: scenarios g * 2048 to (g + 1) * 2048 - 1 have section-three ids g * 128 to (g + 1) * 128 - 1, never falling along the scenarios, every id used. `node_two`: scenarios g * 2048 to (g + 1) * 2048 - 1 have section-two ids g * 32 to (g + 1) * 32 - 1, never falling along the scenarios, every id used; all scenarios of one section-three node share one section-two node.
All inputs are finite; a program needn't handle non-finite values.
Results may differ from a plain program's by a relative error of at most 0.0031.
Values sent between devices are 32-bit elements; how exact they have to be, the bound alone decides.
A program may use at most 64 MiB of HBM per device.

v0:
```python
import jax
import jax.numpy as jnp
from jax import lax
from jax.sharding import PartitionSpec as P

NODE3_GRP = 128
NODE2_GRP = 32
ITERS = 8


admm_sigma = 1.0


def table_rows(labels, count, values, chances):
    onehot = (labels[None, :] == jnp.arange(count, dtype=jnp.int32)[:, None]).astype(jnp.float32)
    sums = jnp.dot(
        onehot, values, precision=lax.Precision.HIGHEST, preferred_element_type=jnp.float32
    )
    totals = jnp.dot(
        onehot, chances, precision=lax.Precision.HIGHEST, preferred_element_type=jnp.float32
    )
    return (onehot, sums, totals)


def spread_back(onehot, means):
    return lax.dot_general(
        onehot,
        means,
        (((0,), (0,)), ((), ())),
        precision=lax.Precision.HIGHEST,
        preferred_element_type=jnp.float32,
    )


def on_device(
    kkt_inverse, cost, anchor, capacity, multiplier, penalty, weight, node_two, node_three
):
    section_width = multiplier.shape[1] // 3
    scen_rows = cost.shape[0]
    padded = jnp.concatenate(
        [multiplier, jnp.zeros((scen_rows, section_width), jnp.float32)], axis=1
    )
    linear = cost + padded - penalty[None, :] * anchor
    box = jnp.clip(anchor, 0.0, capacity)
    scaled = jnp.zeros_like(box)
    for iteration in range(ITERS):
        rhs_value = (admm_sigma * (box - scaled) - linear).astype(jnp.bfloat16)
        trial = jnp.dot(rhs_value, kkt_inverse, preferred_element_type=jnp.float32)
        box = jnp.clip(trial + scaled, 0.0, capacity)
        scaled = scaled + trial - box
    chances = weight.astype(jnp.float32)
    weighted = chances[:, None] * box
    first_cols = weighted[:, :section_width]
    second_cols = weighted[:, section_width : 2 * section_width]
    third_cols = weighted[:, 2 * section_width : 3 * section_width]
    branch_count = lax.axis_size("branch")
    count_three = NODE3_GRP * branch_count
    count_two = NODE2_GRP * branch_count
    onehot_three, sums_three, totals_three = table_rows(
        node_three, count_three, third_cols, chances
    )
    onehot_two, sums_two, totals_two = table_rows(node_two, count_two, second_cols, chances)
    sums_first = jnp.dot(
        onehot_two, first_cols, precision=lax.Precision.HIGHEST, preferred_element_type=jnp.float32
    )
    node_sums = jnp.concatenate([sums_three, sums_two, sums_first], axis=0)
    node_totals = jnp.concatenate([totals_three, totals_two, totals_two], axis=0)
    first_start = count_three + count_two
    node_sums, node_totals = lax.psum((node_sums, node_totals), ("branch", "slot"))
    node_means = node_sums / node_totals[:, None]
    root_sum = jnp.sum(node_sums[first_start:], axis=0)
    root_weight = jnp.sum(node_totals[first_start:])
    root_mean = root_sum / root_weight
    root_rows = jnp.broadcast_to(root_mean[None, :], (scen_rows, section_width))
    second_rows = spread_back(onehot_two, node_means[count_three:first_start])
    third_rows = spread_back(onehot_three, node_means[:count_three])
    consensus = jnp.concatenate([root_rows, second_rows, third_rows], axis=1)
    new_multiplier = multiplier + penalty[None, : 3 * section_width] * (
        box[:, : 3 * section_width] - consensus
    )
    return (box, new_multiplier)


def solution(mesh):
    placed = (
        P(),
        P(("branch", "slot"), None),
        P(("branch", "slot"), None),
        P(("branch", "slot"), None),
        P(("branch", "slot"), None),
        P(),
        P(("branch", "slot")),
        P(("branch", "slot")),
        P(("branch", "slot")),
    )
    return jax.shard_map(
        on_device,
        mesh=mesh,
        in_specs=placed,
        out_specs=(P(("branch", "slot"), None), P(("branch", "slot"), None)),
        check_vma=False,
    )
```

profile of v0, /device:TPU:1, one launch (start us, length us, event | category | flops | bytes accessed | tf_op | source)
XLA Modules:
  0.0 311.3 jit_solution(4172316415720779847)
XLA Ops:
  7.2 0.0 copy-start.1
  7.2 0.0 all-reduce.3.cloned.1.call-start
  7.2 0.0 copy-start
  7.2 0.8 convert_element_type.37
  8.0 1.8 multiply_subtract_fusion
  9.8 5.6 %fusion.31 = f32[64,2048]{1,0:T(8,128)S(1)} fusion(bf16[2048,2048]{1,0:T(8,128)(2,1)} %param.9, f32[64,2048]{1,0:T(8,128)S(1)} %multiply_subtract_fusion, f32[64,2048]{1,0:T(8,128)} %param.12, f32[64,2048]{1,0:T(8,128)} %param.11), kind=kOutput, calls=%fused_computation.52 | convolution fusion | flops 537395200 | bytes 10485760 | tf_op jit(solution)/shard_map/dot_general | solution.py:48
  15.5 1.6 convolution_add_fusion.6
  17.1 1.6 convolution_add_fusion.5
  18.8 1.6 convolution_add_fusion.4
  20.4 1.6 convolution_add_fusion.3
  22.0 1.6 convolution_add_fusion.2
  23.7 1.6 convolution_add_fusion.1
  25.3 0.0 copy-start.6
  25.3 1.7 broadcast_multiply_fusion
  27.1 0.0 copy-start.2
  27.1 0.4 fusion.43
  27.5 0.4 fusion.45
  27.9 1.0 fusion.7
  28.9 0.0 copy-start.3
  28.9 2.0 pad_maximum_fusion
  30.9 0.0 all-reduce.3.cloned.1.call-update
  30.9 0.1 fusion.48
  31.1 0.6 fusion.6
  31.7 82.2 %psum.15 = f32[1536]{0:T(1024)S(1)} all-reduce(f32[1536]{0:T(1024)S(1)} %pad_maximum_fusion.1), channel_id=1, replica_groups=mesh['branch'=8,'slot'=32] {'branch','slot'}, use_global_device_ids=true, to_apply=%region_2.3 | all-reduce | flops 1536 | bytes 12288 | tf_op jit(solution)/shard_map/psum | solution.py:69
  113.8 0.6 slice_reduce_fusion.1
  114.4 183.9 %all-reduce.3.cloned.1.call-done = f32[1536,512]{1,0:T(8,128)} async-done(((f32[1536,512]{1,0:T(8,128)}), f32[1536,512]{1,0:T(8,128)}) %all-reduce.3.cloned.1.call-update) | async-done | bytes 3145744 | tf_op jit(solution)/shard_map/psum | solution.py:69
  298.4 2.2 broadcast_divide_fusion
  300.5 0.9 fusion.2
  301.5 0.3 fusion.4
  301.8 1.1 slice_reduce_fusion
  302.9 0.6 broadcast_divide_fusion.1
  303.6 0.8 fusion.30
  (13 shorter events, 0.0 us)
Async XLA Ops:
  7.2 8.3 %copy-start.1 = (f32[64,2048]{1,0:T(8,128)S(1)}, f32[64,2048]{1,0:T(8,128)}, u32[]{:S(2)}) copy-start(f32[64,2048]{1,0:T(8,128)} %param.12) | copy-start | bytes 1572868
  7.2 291.2 %all-reduce.3.cloned.1.call-start = ((), (), s32[]{:S(2)}) async-start(), calls=%async_computation | async-start | bytes 6291456 | tf_op jit(solution)/shard_map/psum | solution.py:69
  7.2 8.3 %copy-start = (bf16[2048,2048]{1,0:T(8,128)(2,1)S(1)}, bf16[2048,2048]{1,0:T(8,128)(2,1)}, u32[]{:S(2)}) copy-start(bf16[2048,2048]{1,0:T(8,128)(2,1)} %param.9) | copy-start | bytes 25165828
  25.3 1.8 copy-start.5
  25.3 2.5 copy-start.6
  27.1 276.5 %copy-start.2 = (f32[64,2048]{1,0:T(8,128)}, f32[64,2048]{1,0:T(8,128)S(1)}, u32[]{:S(2)}) copy-start(f32[64,2048]{1,0:T(8,128)S(1)} %get-tuple-element.3) | copy-start | bytes 1572868
  27.1 3.8 %copy-start.7 = (s32[64]{0:T(128)S(1)}, s32[64]{0:T(128)}, u32[]{:S(2)}) copy-start(s32[64]{0:T(128)} %param.15) | copy-start | bytes 772
  28.9 274.7 %copy-start.3 = (f32[64,1536]{1,0:T(8,128)S(1)}, f32[64,1536]{1,0:T(8,128)}, u32[]{:S(2)}) copy-start(f32[64,1536]{1,0:T(8,128)} %param.13) | copy-start | bytes 1179652
  28.9 274.7 %copy-start.4 = (f32[2048]{0:T(1024)S(1)}, f32[2048]{0:T(1024)}, u32[]{:S(2)}) copy-start(f32[2048]{0:T(1024)} %param.14) | copy-start | bytes 24580
Sparse Core Ops, SparseCore 0:
  31.1 267.2 all-reduce.2
where the time goes:
time: 312 us; the launch traced here: 311 us
  waiting for transfers between devices  184 us (59%)
  blocking collectives  82.2 us (26%)
  matrix products  20.9 us (7%)
  between operations  14.2 us (5%)
  other arithmetic  9.93 us (3%)
    psum x1, waiting for transfers between devices, on_device(): lax.psum((node_sums, node_totals), ('branch', 'slot'))  184 us
    psum x1, blocking collectives, on_device(): lax.psum((node_sums, node_totals), ('branch', 'slot'))  82.2 us
    dot_general x8, matrix products, on_device(): trial = jnp.dot(rhs_value, kkt_inverse, preferred_element_type=jnp.float32)  17.2 us
  transfers between devices with their start and end apart: 1, of which 1 were waited for; matrix products, arithmetic and copies ran while one was open for 0% of the time, Pallas kernels for 0%

commit v1 on v0

v1 whole, which is shorter than its diff:
```python
import functools

import jax
import jax.numpy as jnp
from jax import lax
from jax.experimental import pallas as pl
from jax.experimental.pallas import tpu as pltpu
from jax.sharding import PartitionSpec as P

ITERS = 8
ROWS = 64
NV = 2048
SEC = 512
BLK = 256
NBLK = NV // BLK
NX, NY, NZ, NC = 4, 4, 8, 2
F32 = jnp.float32
BF16 = jnp.bfloat16
ORDER = (2, 3, 4, 5, 0, 1, 6, 7)


def split2(v):
    hi = v.astype(BF16)
    lo = (v - hi.astype(F32)).astype(BF16)
    return hi, lo


def stack3(v):
    hi, lo = split2(v)
    rest = (v - hi.astype(F32) - lo.astype(F32)).astype(BF16)
    return jnp.concatenate([hi, lo, rest], axis=0)


def mm(a, b):
    return jnp.dot(a, b, preferred_element_type=F32)


def triple(a):
    a = a.astype(BF16)
    return jnp.concatenate([a, a, a], axis=1)


def wait_bytes(ref, sem):
    pltpu.make_async_copy(ref, ref, sem).wait()


def kernel(
    k_h, cost_h, anchor_h, cap_h, mult_h, pen_h, w_h, n2_h, n3_h,
    sol_h, nm_h,
    kv, cost, anchor, cap, mult, pen, wv, n2v, n3v,
    lin, sc, box, rhs, nm,
    coef_a, coef_l, coef_w, coef_c, coef_d, inv,
    meta1, meta1_in, meta2, meta2_in,
    pay1, pay1_in, pay2, pay2_in,
    root1, root1_in, root2, root2_in,
    in_sem, k_sem, out_sem, send_sem, recv_sem,
):
    slot = lax.axis_index("slot")
    branch = lax.axis_index("branch")
    x, z = slot // NZ, slot % NZ
    y, core = branch // NC, branch % NC

    z_peers = [{"slot": x * NZ + (z + d) % NZ} for d in range(1, NZ)]
    x_peers = [{"slot": ((x + d) % NX) * NZ + z} for d in range(1, NX)]
    zc_peers = [
        {"slot": x * NZ + (z + d) % NZ, "branch": y * NC + (core + e) % NC}
        for d in range(NZ) for e in range(NC) if d or e
    ]
    xy_peers = [
        {"slot": ((x + d) % NX) * NZ + z, "branch": ((y + e) % NY) * NC + core}
        for d in range(NX) for e in range(NY) if d or e
    ]

    ins = [
        pltpu.make_async_copy(a, b, in_sem.at[i])
        for i, (a, b) in enumerate((
            (cost_h, cost), (anchor_h, anchor), (mult_h, mult), (pen_h, pen), (cap_h, cap),
            (w_h, wv), (n2_h, n2v), (n3_h, n3v),
        ))
    ]
    for c in ins:
        c.start()
    ks = [
        pltpu.make_async_copy(
            k_h.at[:, pl.ds(j * BLK, BLK)], kv.at[:, pl.ds(j * BLK, BLK)], k_sem.at[j]
        )
        for j in range(NBLK)
    ]
    for c in ks:
        c.start()

    barrier = pltpu.get_barrier_semaphore()
    for peer in zc_peers + xy_peers:
        pl.semaphore_signal(barrier, inc=1, device_id=peer, device_id_type=pl.DeviceIdType.MESH)

    def gather_start(src, dst, peers, index):
        for peer in peers:
            pltpu.make_async_remote_copy(
                src_ref=src, dst_ref=dst, send_sem=send_sem.at[index], recv_sem=recv_sem.at[index],
                device_id=peer, device_id_type=pl.DeviceIdType.MESH,
            ).start()

    for c in ins:
        c.wait()

    start = jnp.clip(anchor[...], 0.0, cap[...])
    lin[:, : 3 * SEC] = (
        cost[:, : 3 * SEC] + mult[...] - pen[:, : 3 * SEC] * anchor[:, : 3 * SEC]
    )
    lin[:, 3 * SEC :] = cost[:, 3 * SEC :] - pen[:, 3 * SEC :] * anchor[:, 3 * SEC :]
    sc[...] = jnp.zeros((ROWS, NV), F32)
    rhs[0] = (start - lin[...]).astype(BF16)

    def block(j, cur, nxt, last):
        s = slice(j * BLK, (j + 1) * BLK)
        trial = jnp.dot(rhs[cur], kv[:, s], preferred_element_type=F32)
        total = trial + sc[:, s]
        new = jnp.clip(total, 0.0, cap[:, s])
        if last:
            box[:, s] = new
            return new
        rest = total - new
        sc[:, s] = rest
        rhs[nxt, :, s] = ((new - rest) - lin[:, s]).astype(BF16)
        return new

    def step(i):
        for j in range(NBLK):
            if i == 0:
                ks[j].wait()
            block(j, i % 2, 1 - i % 2, False)

    step(0)

    w_row = wv[...].astype(F32)
    ids = (n2v[...].astype(F32), n3v[...].astype(F32))
    eye = lax.broadcasted_iota(jnp.int32, (ROWS, ROWS), 0) == lax.broadcasted_iota(
        jnp.int32, (ROWS, ROWS), 1
    )
    sub = lax.broadcasted_iota(jnp.int32, (8, ROWS), 0)
    lane = lax.broadcasted_iota(jnp.int32, (8, 128), 1)
    row8 = lax.broadcasted_iota(jnp.int32, (8, 128), 0)
    id_cols, local_totals, ends = [], [], []
    for t in range(2):
        id_col = jnp.sum(jnp.where(eye, ids[t], 0.0), axis=1, keepdims=True)
        id_cols.append(id_col)
        same = jnp.where(id_col == ids[t], w_row, 0.0)
        coef_l[t] = triple(same)
        local_totals.append(jnp.sum(same, axis=1, keepdims=True))
        first, final = ids[t][:, 0:1], ids[t][:, ROWS - 1 : ROWS]
        at_first = jnp.where(ids[t] == first, w_row, 0.0)
        at_final = jnp.where((ids[t] == final) & (final != first), w_row, 0.0)
        ends.append((first, final, jnp.sum(at_first, axis=1, keepdims=True),
                     jnp.sum(at_final, axis=1, keepdims=True)))
        for h in range(2):
            q = 4 * h + 2 * t
            rows = jnp.where(sub == q, at_first, jnp.where(sub == q + 1, at_final, 0.0))
            coef_a[2 * t + h] = triple(rows)
    for h in range(2):
        coef_w[h] = triple(jnp.where((sub == 2 * h) | (sub == 2 * h + 1), w_row, 0.0))
    weight_sum = jnp.sum(w_row, axis=1, keepdims=True)

    q_lane = lane % 4
    own_ids = jnp.where(
        q_lane == 0, ends[0][0], jnp.where(q_lane == 1, ends[0][1],
        jnp.where(q_lane == 2, ends[1][0], ends[1][1])))
    own_weights = jnp.where(
        q_lane == 0, ends[0][2], jnp.where(q_lane == 1, ends[0][3],
        jnp.where(q_lane == 2, ends[1][2], ends[1][3])))
    message = jnp.where(row8 == 0, own_ids, jnp.where(row8 == 1, own_weights, 0.0))
    message = jnp.where((lane < 64) & (lane // 8 == z), message, 0.0)
    meta1[...] = message
    meta1_in[z] = message

    pl.semaphore_wait(barrier, len(zc_peers) + len(xy_peers))
    gather_start(meta1, meta1_in.at[z], z_peers, 0)
    step(1)
    step(2)

    wait_bytes(meta1_in.at[pl.ds(0, NZ - 1)], recv_sem.at[0])
    line = jnp.sum(meta1_in[...], axis=0)
    line_ids, line_w = line[0:1], line[1:2]
    odd = row8 % 2 == 1
    targ = jnp.sum(
        jnp.where(lane == row8 + jnp.where(odd, 56, 0), line_ids, 0.0), axis=1, keepdims=True
    )
    before = jnp.sum(jnp.where(lane == row8 - 1, line_ids, 0.0), axis=1, keepdims=True)
    group = (lane < 64) & ((lane % 8) // 2 == row8 // 2)
    keep = jnp.logical_not(odd) | (targ != before)
    spread = jnp.where(group & keep & (line_ids == targ), 1.0, 0.0)
    line_weight = jnp.sum(spread * line_w, axis=1, keepdims=True)
    place = lane == 64 + x * 8 + row8
    put_ids = jnp.sum(jnp.where(place, targ, 0.0), axis=0, keepdims=True)
    put_w = jnp.sum(jnp.where(place, line_weight, 0.0), axis=0, keepdims=True)
    message = jnp.where(row8 == 0, put_ids, jnp.where(row8 == 1, put_w, 0.0))
    meta2[...] = message
    meta2_in[x] = message
    coef_d[...] = (spread + pltpu.roll(spread, 64, 1)).astype(BF16)
    gather_start(meta2, meta2_in.at[x], x_peers, 1)
    step(3)
    step(4)

    wait_bytes(meta2_in.at[pl.ds(0, NX - 1)], recv_sem.at[1])
    table = line + jnp.sum(meta2_in[...], axis=0)
    all_ids, all_w = table[0:1], table[1:2]
    wide = lax.broadcasted_iota(jnp.int32, (ROWS, 128), 1)
    other = ((wide < 64) & (wide // 8 != z)) | (
        (wide >= 64) & (wide < 96) & ((wide - 64) // 8 != x)
    )
    for t in range(2):
        match = (id_cols[t] == all_ids) & other & ((wide % 4) // 2 == t)
        for h in range(2):
            part = jnp.where(match & ((wide % 8) // 4 == h), 1.0, 0.0)
            if h == 0:
                total = local_totals[t] + jnp.sum(part * all_w, axis=1, keepdims=True)
                inv[:, 128 * t : 128 * t + 128] = jnp.broadcast_to(1.0 / total, (ROWS, 128))
            half = part.astype(BF16)
            q = 2 * t + h
            coef_c[q * ROWS : (q + 1) * ROWS] = jnp.concatenate([half, half], axis=1)
    step(5)
    step(6)

    outs = []
    nodes = jnp.zeros((8, BLK), F32)
    roots = jnp.where(row8 == 4, weight_sum, 0.0)
    for n, j in enumerate(ORDER):
        new = block(j, 1, 0, True)
        s = pl.ds(j * BLK, BLK)
        out = pltpu.make_async_copy(box.at[:, s], sol_h.at[:, s], out_sem.at[j])
        out.start()
        outs.append(out)
        if j < 2:
            part = mm(coef_w[j], stack3(new))
            roots = jnp.where(row8 == 2 * j, part[:, :128], roots)
            roots = jnp.where(row8 == 2 * j + 1, part[:, 128:], roots)
            if j == 1:
                root1[...] = roots
                root1_in[z * NC + core] = roots
                gather_start(root1, root1_in.at[z * NC + core], zc_peers, 4)
        elif j < 6:
            nodes = nodes + mm(coef_a[j - 2], stack3(new))
            if j == 5:
                pay1[...] = nodes
                pay1_in[z] = nodes
                gather_start(pay1, pay1_in.at[z], z_peers, 2)

    for t in range(2):
        for h in range(2):
            c = SEC * (t + 1) + BLK * h
            s = slice(c, c + BLK)
            local = mm(coef_l[t], stack3(box[:, s]))
            scale = inv[:, 128 * t : 128 * t + 1]
            nm[:, s] = mult[:, s] + pen[:, s] * (box[:, s] - local * scale)
    nm[:, :SEC] = mult[:, :SEC] + pen[:, :SEC] * box[:, :SEC]

    wait_bytes(pay1_in.at[pl.ds(0, NZ - 1)], recv_sem.at[2])
    hi1, lo1 = split2(pay1_in[...].reshape(NZ * 8, BLK))
    nodes = mm(coef_d[...], jnp.concatenate([hi1, lo1], axis=0))
    pay2[...] = nodes
    pay2_in[x] = nodes
    gather_start(pay2, pay2_in.at[x], x_peers, 3)

    wait_bytes(root1_in.at[pl.ds(0, NZ * NC - 1)], recv_sem.at[4])
    roots = jnp.sum(root1_in[...], axis=0)
    root2[...] = roots
    root2_in[x * NY + y] = roots
    gather_start(root2, root2_in.at[x * NY + y], xy_peers, 5)

    wait_bytes(pay2_in.at[pl.ds(0, NX - 1)], recv_sem.at[3])
    hi2, lo2 = split2(pay2_in[...].reshape(NX * 8, BLK))
    none = jnp.zeros((32, BLK), BF16)
    stacked = jnp.concatenate([hi1, hi2, none, lo1, lo2, none], axis=0)
    remote = mm(coef_c[...], stacked)
    for t in range(2):
        for h in range(2):
            c = SEC * (t + 1) + BLK * h
            s = slice(c, c + BLK)
            q = 2 * t + h
            scale = inv[:, 128 * t : 128 * t + 1]
            nm[:, s] = nm[:, s] - pen[:, s] * (remote[q * ROWS : (q + 1) * ROWS] * scale)
    out = pltpu.make_async_copy(
        nm.at[:, pl.ds(SEC, 2 * SEC)], nm_h.at[:, pl.ds(SEC, 2 * SEC)], out_sem.at[NBLK]
    )
    out.start()
    outs.append(out)

    wait_bytes(root2_in.at[pl.ds(0, NX * NY - 1)], recv_sem.at[5])
    roots = jnp.sum(root2_in[...], axis=0)
    means = roots / roots[4:5]
    for r in range(4):
        s = slice(128 * r, 128 * r + 128)
        nm[:, s] = nm[:, s] - pen[:, s] * means[r : r + 1]
    out = pltpu.make_async_copy(
        nm.at[:, pl.ds(0, SEC)], nm_h.at[:, pl.ds(0, SEC)], out_sem.at[NBLK + 1]
    )
    out.start()
    outs.append(out)

    for index, ref in enumerate((
        meta1_in.at[pl.ds(0, NZ - 1)], meta2_in.at[pl.ds(0, NX - 1)],
        pay1_in.at[pl.ds(0, NZ - 1)], pay2_in.at[pl.ds(0, NX - 1)],
        root1_in.at[pl.ds(0, NZ * NC - 1)], root2_in.at[pl.ds(0, NX * NY - 1)],
    )):
        wait_bytes(ref, send_sem.at[index])
    for out in outs:
        out.wait()


def on_device(
    kkt_inverse, cost, anchor, capacity, multiplier, penalty, weight, node_two, node_three
):
    anywhere = pl.BlockSpec(memory_space=pl.ANY)
    vm = pltpu.VMEM
    return pl.pallas_call(
        kernel,
        out_shape=(
            jax.ShapeDtypeStruct((ROWS, NV), F32),
            jax.ShapeDtypeStruct((ROWS, 3 * SEC), F32),
        ),
        in_specs=[anywhere] * 9,
        out_specs=(anywhere, anywhere),
        scratch_shapes=[
            vm((NV, NV), BF16), vm((ROWS, NV), F32), vm((ROWS, NV), F32), vm((ROWS, NV), F32),
            vm((ROWS, 3 * SEC), F32), vm((1, NV), F32),
            vm((1, ROWS), jnp.int32), vm((1, ROWS), jnp.int32), vm((1, ROWS), jnp.int32),
            vm((ROWS, NV), F32), vm((ROWS, NV), F32), vm((ROWS, NV), F32),
            vm((2, ROWS, NV), BF16), vm((ROWS, 3 * SEC), F32),
            vm((4, 8, 192), BF16), vm((2, ROWS, 192), BF16), vm((2, 8, 192), BF16),
            vm((4 * ROWS, 256), BF16), vm((8, 128), BF16), vm((ROWS, 256), F32),
            vm((8, 128), F32), vm((NZ, 8, 128), F32), vm((8, 128), F32), vm((NX, 8, 128), F32),
            vm((8, BLK), F32), vm((NZ, 8, BLK), F32), vm((8, BLK), F32), vm((NX, 8, BLK), F32),
            vm((8, 128), F32), vm((NZ * NC, 8, 128), F32),
            vm((8, 128), F32), vm((NX * NY, 8, 128), F32),
            pltpu.SemaphoreType.DMA((8,)), pltpu.SemaphoreType.DMA((NBLK,)),
            pltpu.SemaphoreType.DMA((NBLK + 2,)),
            pltpu.SemaphoreType.DMA((6,)), pltpu.SemaphoreType.DMA((6,)),
        ],
        compiler_params=pltpu.CompilerParams(
            collective_id=0, has_side_effects=True, vmem_limit_bytes=64 << 20
        ),
        cost_estimate=pl.CostEstimate(
            flops=2 * ITERS * ROWS * NV * NV, bytes_accessed=12 << 20, transcendentals=0
        ),
    )(
        kkt_inverse, cost, anchor, capacity, multiplier, penalty.reshape(1, NV),
        weight.reshape(1, ROWS), node_two.reshape(1, ROWS), node_three.reshape(1, ROWS),
    )


def solution(mesh):
    rows = P(("branch", "slot"), None)
    flat = P(("branch", "slot"))
    return jax.shard_map(
        on_device,
        mesh=mesh,
        in_specs=(P(), rows, rows, rows, rows, P(), flat, flat, flat),
        out_specs=(rows, rows),
        check_vma=False,
    )
```

time: 312 us -> 41.9 us (0.13)
  waiting for transfers between devices: 184 us -> 0 us
  blocking collectives: 82.2 us -> 0 us
  Pallas kernels: 0 us -> 37.4 us
  matrix products: 20.9 us -> 0 us
  between operations: 14.2 us -> 0.64 us
  other arithmetic: 9.93 us -> 0 us
  local copies, waits for them, and re-layouts: 0.05 us -> 3.64 us
    psum x1 -> x0, waiting for transfers between devices: 184 us -> none  [on_device(): lax.psum((node_sums, node_totals), ('branch', 'slot'))]
    psum x1 -> x0, blocking collectives: 82.2 us -> none  [on_device(): lax.psum((node_sums, node_totals), ('branch', 'slot'))]
    pallas_call x0 -> x1, Pallas kernels: none -> 37.4 us  [on_device(): pl.pallas_call(kernel, out_shape=(jax.ShapeDtypeStruct((ROWS, NV), F32),...]
    dot_general x15 -> x0, matrix products: 20.9 us -> none  [the longest x8 17.2 us: on_device(): trial = jnp.dot(rhs_value, kkt_inverse, preferred_element_type=jnp.float32)]
    unnamed x16 -> x2, local copies, waits for them, and re-layouts: 0.05 us -> 3.64 us
  transfers between devices with their start and end apart: 1 -> 0, of which waited for: 1 -> 0; matrix products, arithmetic and copies ran while one was open for 0% -> 0% of each run, Pallas kernels for 0% -> 0%
where the time goes in v1:
time: 41.9 us; the launch traced here: 41.7 us
  Pallas kernels  37.4 us (89%)
  local copies, waits for them, and re-layouts  3.64 us (9%)
  between operations  0.64 us (2%)
    pallas_call x1, Pallas kernels, on_device(): pl.pallas_call(kernel, out_shape=(jax.ShapeDtypeStruct((ROWS, NV), F32),...  37.4 us
    unnamed x2, local copies, waits for them, and re-layouts  3.64 us

profile of v1, /device:TPU:1, one launch (start us, length us, event | category | flops | bytes accessed | tf_op | source)
XLA Modules:
  0.0 41.7 jit_solution(4007665342327708846)
XLA Ops:
  0.6 37.4 %shard_map.104 = (f32[64,2048]{1,0:T(8,128)}, f32[64,1536]{1,0:T(8,128)}) custom-call(bf16[2048,2048]{1,0:T(8,128)(2,1)} %k_h.1, f32[64,2048]{1,0:T(8,128)} %cost_h.1, f32[64,2048]{1,0:T(8,128)} %anchor_h.1, f32[64,2048]{1,0:T(8,128)} %cap_h.1, f32[64,1536]{1,0:T(8,128)} %mult_h.1, f32[1,2048]{1,0:T(1,128)} %bitcast.4, s32[1,64]{1,0:T(1,128)} %bitcast.5, ...), custom_call_target="tpu_custom_call" | custom-call | flops 4294967296 | bytes 12582912 | tf_op jit(solution)/shard_map/pallas_call | solution.py:314
  38.1 1.9 %copy.13 = f32[64,2048]{1,0:T(8,128)} copy(f32[64,2048]{1,0:T(8,128)} %get-tuple-element.4) | data formatting | bytes 1048576
  39.9 1.8 %copy.14 = f32[64,1536]{1,0:T(8,128)} copy(f32[64,1536]{1,0:T(8,128)} %get-tuple-element.5) | data formatting | bytes 786432

commit v2 on v1

--- a/solution.py
+++ b/solution.py
@@ -16,7 +16,10 @@
 NX, NY, NZ, NC = 4, 4, 8, 2
 F32 = jnp.float32
 BF16 = jnp.bfloat16
-ORDER = (2, 3, 4, 5, 0, 1, 6, 7)
+XY_FAR_FIRST = (
+    (2, 2), (2, 1), (2, 3), (1, 2), (3, 2), (2, 0), (0, 2), (1, 1), (1, 3), (3, 1), (3, 3),
+    (1, 0), (3, 0), (0, 1), (0, 3),
+)
 
 
 def split2(v):
@@ -46,30 +49,28 @@
 
 def kernel(
     k_h, cost_h, anchor_h, cap_h, mult_h, pen_h, w_h, n2_h, n3_h,
-    sol_h, nm_h,
+    box, nm,
     kv, cost, anchor, cap, mult, pen, wv, n2v, n3v,
-    lin, sc, box, rhs, nm,
-    coef_a, coef_l, coef_w, coef_c, coef_d, inv,
+    lin, sc, rhs,
+    coef_l, coef_c, coef_d, mask, inv,
     meta1, meta1_in, meta2, meta2_in,
     pay1, pay1_in, pay2, pay2_in,
-    root1, root1_in, root2, root2_in,
-    in_sem, k_sem, out_sem, send_sem, recv_sem,
+    root1, root1_in, root2, root2_in, root3, root3_in,
+    in_sem, k_sem, send_sem, recv_sem,
 ):
     slot = lax.axis_index("slot")
     branch = lax.axis_index("branch")
     x, z = slot // NZ, slot % NZ
     y, core = branch // NC, branch % NC
 
-    z_peers = [{"slot": x * NZ + (z + d) % NZ} for d in range(1, NZ)]
-    x_peers = [{"slot": ((x + d) % NX) * NZ + z} for d in range(1, NX)]
-    zc_peers = [
-        {"slot": x * NZ + (z + d) % NZ, "branch": y * NC + (core + e) % NC}
-        for d in range(NZ) for e in range(NC) if d or e
-    ]
+    z_peers = [{"slot": x * NZ + (z + d) % NZ} for d in (4, 3, 5, 2, 6, 1, 7)]
+    x_peers = [{"slot": ((x + d) % NX) * NZ + z} for d in (2, 1, 3)]
     xy_peers = [
         {"slot": ((x + d) % NX) * NZ + z, "branch": ((y + e) % NY) * NC + core}
-        for d in range(NX) for e in range(NY) if d or e
+        for d, e in XY_FAR_FIRST
     ]
+    c_peers = [{"branch": y * NC + 1 - core}]
+    peers = z_peers + xy_peers + c_peers
 
     ins = [
         pltpu.make_async_copy(a, b, in_sem.at[i])
@@ -90,8 +91,14 @@
         c.start()
 
     barrier = pltpu.get_barrier_semaphore()
-    for peer in zc_peers + xy_peers:
-        pl.semaphore_signal(barrier, inc=1, device_id=peer, device_id_type=pl.DeviceIdType.MESH)
+
+    def greet(some):
+        for peer in some:
+            pl.semaphore_signal(
+                barrier, inc=1, device_id=peer, device_id_type=pl.DeviceIdType.MESH
+            )
+
+    greet(peers[:8])
 
     def gather_start(src, dst, peers, index):
         for peer in peers:
@@ -127,6 +134,7 @@
     def step(i):
         for j in range(NBLK):
             if i == 0:
+                greet(peers[8 + 2 * j : 10 + 2 * j])
                 ks[j].wait()
             block(j, i % 2, 1 - i % 2, False)
 
@@ -137,7 +145,11 @@
     eye = lax.broadcasted_iota(jnp.int32, (ROWS, ROWS), 0) == lax.broadcasted_iota(
         jnp.int32, (ROWS, ROWS), 1
     )
-    sub = lax.broadcasted_iota(jnp.int32, (8, ROWS), 0)
+
+    def column(row):
+        col = jnp.sum(jnp.where(eye, row, 0.0), axis=1, keepdims=True)
+        return jnp.broadcast_to(col, (ROWS, 128))
+
     lane = lax.broadcasted_iota(jnp.int32, (8, 128), 1)
     row8 = lax.broadcasted_iota(jnp.int32, (8, 128), 0)
     id_cols, local_totals, ends = [], [], []
@@ -152,12 +164,9 @@
         at_final = jnp.where((ids[t] == final) & (final != first), w_row, 0.0)
         ends.append((first, final, jnp.sum(at_first, axis=1, keepdims=True),
                      jnp.sum(at_final, axis=1, keepdims=True)))
-        for h in range(2):
-            q = 4 * h + 2 * t
-            rows = jnp.where(sub == q, at_first, jnp.where(sub == q + 1, at_final, 0.0))
-            coef_a[2 * t + h] = triple(rows)
-    for h in range(2):
-        coef_w[h] = triple(jnp.where((sub == 2 * h) | (sub == 2 * h + 1), w_row, 0.0))
+        mask[2 * t] = column(at_first)
+        mask[2 * t + 1] = column(at_final)
+    mask[4] = column(w_row)
     weight_sum = jnp.sum(w_row, axis=1, keepdims=True)
 
     q_lane = lane % 4
@@ -172,10 +181,13 @@
     meta1[...] = message
     meta1_in[z] = message
 
-    pl.semaphore_wait(barrier, len(zc_peers) + len(xy_peers))
-    gather_start(meta1, meta1_in.at[z], z_peers, 0)
     step(1)
     step(2)
+    pl.semaphore_wait(barrier, len(peers))
+    gather_start(meta1, meta1_in.at[z], z_peers, 0)
+    step(3)
+    step(4)
+    step(5)
 
     wait_bytes(meta1_in.at[pl.ds(0, NZ - 1)], recv_sem.at[0])
     line = jnp.sum(meta1_in[...], axis=0)
@@ -197,8 +209,36 @@
     meta2_in[x] = message
     coef_d[...] = (spread + pltpu.roll(spread, 64, 1)).astype(BF16)
     gather_start(meta2, meta2_in.at[x], x_peers, 1)
-    step(3)
-    step(4)
+    step(6)
+
+
+    def weighted(new, index):
+        m = mask[index]
+        return [
+            jnp.sum(new[:, 128 * i : 128 * i + 128] * m, axis=0, keepdims=True)
+            for i in range(2)
+        ]
+
+    roots = jnp.where(row8 == 4, weight_sum, 0.0)
+    for j in range(2):
+        for i, part in enumerate(weighted(block(j, 1, 0, True), 4)):
+            roots = jnp.where(row8 == 2 * j + i, part, roots)
+    root1[...] = roots
+    root1_in[z] = roots
+    gather_start(root1, root1_in.at[z], z_peers, 4)
+    halves = [jnp.zeros((8, 128), F32), jnp.zeros((8, 128), F32)]
+    for j in range(2, 6):
+        t, h = (j - 2) // 2, (j - 2) % 2
+        new = block(j, 1, 0, True)
+        for end in range(2):
+            for i, part in enumerate(weighted(new, 2 * t + end)):
+                halves[i] = jnp.where(row8 == 4 * h + 2 * t + end, part, halves[i])
+    nodes = jnp.concatenate(halves, axis=1)
+    pay1[...] = nodes
+    pay1_in[z] = nodes
+    gather_start(pay1, pay1_in.at[z], z_peers, 2)
+    for j in range(6, NBLK):
+        block(j, 1, 0, True)
 
     wait_bytes(meta2_in.at[pl.ds(0, NX - 1)], recv_sem.at[1])
     table = line + jnp.sum(meta2_in[...], axis=0)
@@ -217,32 +257,6 @@
             half = part.astype(BF16)
             q = 2 * t + h
             coef_c[q * ROWS : (q + 1) * ROWS] = jnp.concatenate([half, half], axis=1)
-    step(5)
-    step(6)
-
-    outs = []
-    nodes = jnp.zeros((8, BLK), F32)
-    roots = jnp.where(row8 == 4, weight_sum, 0.0)
-    for n, j in enumerate(ORDER):
-        new = block(j, 1, 0, True)
-        s = pl.ds(j * BLK, BLK)
-        out = pltpu.make_async_copy(box.at[:, s], sol_h.at[:, s], out_sem.at[j])
-        out.start()
-        outs.append(out)
-        if j < 2:
-            part = mm(coef_w[j], stack3(new))
-            roots = jnp.where(row8 == 2 * j, part[:, :128], roots)
-            roots = jnp.where(row8 == 2 * j + 1, part[:, 128:], roots)
-            if j == 1:
-                root1[...] = roots
-                root1_in[z * NC + core] = roots
-                gather_start(root1, root1_in.at[z * NC + core], zc_peers, 4)
-        elif j < 6:
-            nodes = nodes + mm(coef_a[j - 2], stack3(new))
-            if j == 5:
-                pay1[...] = nodes
-                pay1_in[z] = nodes
-                gather_start(pay1, pay1_in.at[z], z_peers, 2)
 
     for t in range(2):
         for h in range(2):
@@ -253,18 +267,18 @@
             nm[:, s] = mult[:, s] + pen[:, s] * (box[:, s] - local * scale)
     nm[:, :SEC] = mult[:, :SEC] + pen[:, :SEC] * box[:, :SEC]
 
+    wait_bytes(root1_in.at[pl.ds(0, NZ - 1)], recv_sem.at[4])
+    roots = jnp.sum(root1_in[...], axis=0)
+    root2[...] = roots
+    root2_in[x * NY + y] = roots
+    gather_start(root2, root2_in.at[x * NY + y], xy_peers, 5)
+
     wait_bytes(pay1_in.at[pl.ds(0, NZ - 1)], recv_sem.at[2])
     hi1, lo1 = split2(pay1_in[...].reshape(NZ * 8, BLK))
     nodes = mm(coef_d[...], jnp.concatenate([hi1, lo1], axis=0))
     pay2[...] = nodes
     pay2_in[x] = nodes
     gather_start(pay2, pay2_in.at[x], x_peers, 3)
-
-    wait_bytes(root1_in.at[pl.ds(0, NZ * NC - 1)], recv_sem.at[4])
-    roots = jnp.sum(root1_in[...], axis=0)
-    root2[...] = roots
-    root2_in[x * NY + y] = roots
-    gather_start(root2, root2_in.at[x * NY + y], xy_peers, 5)
 
     wait_bytes(pay2_in.at[pl.ds(0, NX - 1)], recv_sem.at[3])
     hi2, lo2 = split2(pay2_in[...].reshape(NX * 8, BLK))
@@ -278,32 +292,24 @@
             q = 2 * t + h
             scale = inv[:, 128 * t : 128 * t + 1]
             nm[:, s] = nm[:, s] - pen[:, s] * (remote[q * ROWS : (q + 1) * ROWS] * scale)
-    out = pltpu.make_async_copy(
-        nm.at[:, pl.ds(SEC, 2 * SEC)], nm_h.at[:, pl.ds(SEC, 2 * SEC)], out_sem.at[NBLK]
-    )
-    out.start()
-    outs.append(out)
 
     wait_bytes(root2_in.at[pl.ds(0, NX * NY - 1)], recv_sem.at[5])
     roots = jnp.sum(root2_in[...], axis=0)
+    root3[...] = roots
+    gather_start(root3, root3_in, c_peers, 6)
+    wait_bytes(root3_in, recv_sem.at[6])
+    roots = roots + root3_in[...]
     means = roots / roots[4:5]
     for r in range(4):
         s = slice(128 * r, 128 * r + 128)
         nm[:, s] = nm[:, s] - pen[:, s] * means[r : r + 1]
-    out = pltpu.make_async_copy(
-        nm.at[:, pl.ds(0, SEC)], nm_h.at[:, pl.ds(0, SEC)], out_sem.at[NBLK + 1]
-    )
-    out.start()
-    outs.append(out)
 
     for index, ref in enumerate((
         meta1_in.at[pl.ds(0, NZ - 1)], meta2_in.at[pl.ds(0, NX - 1)],
         pay1_in.at[pl.ds(0, NZ - 1)], pay2_in.at[pl.ds(0, NX - 1)],
-        root1_in.at[pl.ds(0, NZ * NC - 1)], root2_in.at[pl.ds(0, NX * NY - 1)],
+        root1_in.at[pl.ds(0, NZ - 1)], root2_in.at[pl.ds(0, NX * NY - 1)], root3_in,
     )):
         wait_bytes(ref, send_sem.at[index])
-    for out in outs:
-        out.wait()
 
 
 def on_device(
@@ -318,33 +324,35 @@
             jax.ShapeDtypeStruct((ROWS, 3 * SEC), F32),
         ),
         in_specs=[anywhere] * 9,
-        out_specs=(anywhere, anywhere),
+        out_specs=(pl.BlockSpec(memory_space=vm), pl.BlockSpec(memory_space=vm)),
         scratch_shapes=[
             vm((NV, NV), BF16), vm((ROWS, NV), F32), vm((ROWS, NV), F32), vm((ROWS, NV), F32),
             vm((ROWS, 3 * SEC), F32), vm((1, NV), F32),
             vm((1, ROWS), jnp.int32), vm((1, ROWS), jnp.int32), vm((1, ROWS), jnp.int32),
-            vm((ROWS, NV), F32), vm((ROWS, NV), F32), vm((ROWS, NV), F32),
-            vm((2, ROWS, NV), BF16), vm((ROWS, 3 * SEC), F32),
-            vm((4, 8, 192), BF16), vm((2, ROWS, 192), BF16), vm((2, 8, 192), BF16),
-            vm((4 * ROWS, 256), BF16), vm((8, 128), BF16), vm((ROWS, 256), F32),
+            vm((ROWS, NV), F32), vm((ROWS, NV), F32), vm((2, ROWS, NV), BF16),
+            vm((2, ROWS, 192), BF16), vm((4 * ROWS, 256), BF16), vm((8, 128), BF16),
+            vm((5, ROWS, 128), F32), vm((ROWS, 256), F32),
             vm((8, 128), F32), vm((NZ, 8, 128), F32), vm((8, 128), F32), vm((NX, 8, 128), F32),
             vm((8, BLK), F32), vm((NZ, 8, BLK), F32), vm((8, BLK), F32), vm((NX, 8, BLK), F32),
-            vm((8, 128), F32), vm((NZ * NC, 8, 128), F32),
+            vm((8, 128), F32), vm((NZ, 8, 128), F32),
             vm((8, 128), F32), vm((NX * NY, 8, 128), F32),
+            vm((8, 128), F32), vm((8, 128), F32),
             pltpu.SemaphoreType.DMA((8,)), pltpu.SemaphoreType.DMA((NBLK,)),
-            pltpu.SemaphoreType.DMA((NBLK + 2,)),
-            pltpu.SemaphoreType.DMA((6,)), pltpu.SemaphoreType.DMA((6,)),
+            pltpu.SemaphoreType.DMA((7,)), pltpu.SemaphoreType.DMA((7,)),
         ],
         compiler_params=pltpu.CompilerParams(
-            collective_id=0, has_side_effects=True, vmem_limit_bytes=64 << 20
+            collective_id=0, has_side_effects=True, vmem_limit_bytes=24 << 20
         ),
         cost_estimate=pl.CostEstimate(
             flops=2 * ITERS * ROWS * NV * NV, bytes_accessed=12 << 20, transcendentals=0
         ),
-    )(
-        kkt_inverse, cost, anchor, capacity, multiplier, penalty.reshape(1, NV),
-        weight.reshape(1, ROWS), node_two.reshape(1, ROWS), node_three.reshape(1, ROWS),
-    )
+    )(*(
+        pltpu.with_memory_space_constraint(a, pltpu.HBM)
+        for a in (
+            kkt_inverse, cost, anchor, capacity, multiplier, penalty.reshape(1, NV),
+            weight.reshape(1, ROWS), node_two.reshape(1, ROWS), node_three.reshape(1, ROWS),
+        )
+    ))
 
 
 def solution(mesh):

time: 41.9 us -> 37 us (0.88)
  Pallas kernels: 37.4 us -> 34.8 us
  local copies, waits for them, and re-layouts: 3.64 us -> 1.54 us
    pallas_call x1, Pallas kernels: 37.4 us -> 34.8 us  [on_device(): pl.pallas_call(kernel, out_shape=(jax.ShapeDtypeStruct((ROWS, NV), F32),...]
    unnamed x2, local copies, waits for them, and re-layouts: 3.64 us -> 1.54 us
where the time goes in v2:
time: 37 us; the launch traced here: 36.9 us
  Pallas kernels  34.8 us (94%)
  local copies, waits for them, and re-layouts  1.54 us (4%)
  between operations  0.64 us (2%)
    pallas_call x1, Pallas kernels, on_device(): pl.pallas_call(kernel, out_shape=(jax.ShapeDtypeStruct((ROWS, NV), F32),...  34.8 us
    unnamed x2, local copies, waits for them, and re-layouts  1.54 us

profile of v2, /device:TPU:1, one launch (start us, length us, event | category | flops | bytes accessed | tf_op | source)
XLA Modules:
  0.0 36.9 jit_solution(8293725447973939098)
XLA Ops:
  0.6 34.8 %shard_map.104 = (f32[64,2048]{1,0:T(8,128)S(1)}, f32[64,1536]{1,0:T(8,128)S(1)}) custom-call(bf16[2048,2048]{1,0:T(8,128)(2,1)} %k_h.1, f32[64,2048]{1,0:T(8,128)} %cost_h.1, f32[64,2048]{1,0:T(8,128)} %anchor_h.1, f32[64,2048]{1,0:T(8,128)} %cap_h.1, f32[64,1536]{1,0:T(8,128)} %mult_h.1, f32[1,2048]{1,0:T(1,128)} %bitcast.4, s32[1,64]{1,0:T(1,128)} %bitcast.5, ...), custom_call_target="tpu_custom_call" | custom-call | flops 4294967296 | bytes 12582912 | tf_op jit(solution)/shard_map/pallas_call | solution.py:320
  35.4 0.8 %copy.13 = f32[64,2048]{1,0:T(8,128)} copy(f32[64,2048]{1,0:T(8,128)S(1)} %get-tuple-element.4) | data formatting | bytes 1048576
  36.2 0.7 %copy.14 = f32[64,1536]{1,0:T(8,128)} copy(f32[64,1536]{1,0:T(8,128)S(1)} %get-tuple-element.5) | data formatting | bytes 786432

commit v3 on v2

--- a/solution.py
+++ b/solution.py
@@ -98,7 +98,7 @@
                 barrier, inc=1, device_id=peer, device_id_type=pl.DeviceIdType.MESH
             )
 
-    greet(peers[:8])
+    greet(peers[:10])
 
     def gather_start(src, dst, peers, index):
         for peer in peers:
@@ -117,6 +117,7 @@
     lin[:, 3 * SEC :] = cost[:, 3 * SEC :] - pen[:, 3 * SEC :] * anchor[:, 3 * SEC :]
     sc[...] = jnp.zeros((ROWS, NV), F32)
     rhs[0] = (start - lin[...]).astype(BF16)
+    greet(peers[10:])
 
     def block(j, cur, nxt, last):
         s = slice(j * BLK, (j + 1) * BLK)
@@ -133,9 +134,9 @@
 
     def step(i):
         for j in range(NBLK):
-            if i == 0:
-                greet(peers[8 + 2 * j : 10 + 2 * j])
-                ks[j].wait()
+            if i == 0 and j % 4 == 0:
+                for c in ks[j : j + 4]:
+                    c.wait()
             block(j, i % 2, 1 - i % 2, False)
 
     step(0)

time: 37 us -> 36.2 us (0.978)
  Pallas kernels: 34.8 us -> 33.9 us
    pallas_call x1, Pallas kernels: 34.8 us -> 33.9 us  [on_device(): pl.pallas_call(kernel, out_shape=(jax.ShapeDtypeStruct((ROWS, NV), F32),...]
where the time goes in v3:
time: 36.2 us; the launch traced here: 36.1 us
  Pallas kernels  33.9 us (94%)
  local copies, waits for them, and re-layouts  1.54 us (4%)
  between operations  0.64 us (2%)
    pallas_call x1, Pallas kernels, on_device(): pl.pallas_call(kernel, out_shape=(jax.ShapeDtypeStruct((ROWS, NV), F32),...  33.9 us
    unnamed x2, local copies, waits for them, and re-layouts  1.54 us

profile of v3, /device:TPU:1, one launch (start us, length us, event | category | flops | bytes accessed | tf_op | source)
XLA Modules:
  0.0 36.1 jit_solution(8230566490873368929)
XLA Ops:
  0.6 33.9 %shard_map.104 = (f32[64,2048]{1,0:T(8,128)S(1)}, f32[64,1536]{1,0:T(8,128)S(1)}) custom-call(bf16[2048,2048]{1,0:T(8,128)(2,1)} %k_h.1, f32[64,2048]{1,0:T(8,128)} %cost_h.1, f32[64,2048]{1,0:T(8,128)} %anchor_h.1, f32[64,2048]{1,0:T(8,128)} %cap_h.1, f32[64,1536]{1,0:T(8,128)} %mult_h.1, f32[1,2048]{1,0:T(1,128)} %bitcast.4, s32[1,64]{1,0:T(1,128)} %bitcast.5, ...), custom_call_target="tpu_custom_call" | custom-call | flops 4294967296 | bytes 12582912 | tf_op jit(solution)/shard_map/pallas_call | solution.py:321
  34.5 0.8 %copy.13 = f32[64,2048]{1,0:T(8,128)} copy(f32[64,2048]{1,0:T(8,128)S(1)} %get-tuple-element.4) | data formatting | bytes 1048576
  35.3 0.7 %copy.14 = f32[64,1536]{1,0:T(8,128)} copy(f32[64,1536]{1,0:T(8,128)S(1)} %get-tuple-element.5) | data formatting | bytes 786432

commit v4 on v3

--- a/solution.py
+++ b/solution.py
@@ -241,6 +241,12 @@
     for j in range(6, NBLK):
         block(j, 1, 0, True)
 
+    wait_bytes(root1_in.at[pl.ds(0, NZ - 1)], recv_sem.at[4])
+    roots = jnp.sum(root1_in[...], axis=0)
+    root2[...] = roots
+    root2_in[x * NY + y] = roots
+    gather_start(root2, root2_in.at[x * NY + y], xy_peers, 5)
+
     wait_bytes(meta2_in.at[pl.ds(0, NX - 1)], recv_sem.at[1])
     table = line + jnp.sum(meta2_in[...], axis=0)
     all_ids, all_w = table[0:1], table[1:2]
@@ -268,18 +274,17 @@
             nm[:, s] = mult[:, s] + pen[:, s] * (box[:, s] - local * scale)
     nm[:, :SEC] = mult[:, :SEC] + pen[:, :SEC] * box[:, :SEC]
 
-    wait_bytes(root1_in.at[pl.ds(0, NZ - 1)], recv_sem.at[4])
-    roots = jnp.sum(root1_in[...], axis=0)
-    root2[...] = roots
-    root2_in[x * NY + y] = roots
-    gather_start(root2, root2_in.at[x * NY + y], xy_peers, 5)
-
     wait_bytes(pay1_in.at[pl.ds(0, NZ - 1)], recv_sem.at[2])
     hi1, lo1 = split2(pay1_in[...].reshape(NZ * 8, BLK))
     nodes = mm(coef_d[...], jnp.concatenate([hi1, lo1], axis=0))
     pay2[...] = nodes
     pay2_in[x] = nodes
     gather_start(pay2, pay2_in.at[x], x_peers, 3)
+
+    wait_bytes(root2_in.at[pl.ds(0, NX * NY - 1)], recv_sem.at[5])
+    roots = jnp.sum(root2_in[...], axis=0)
+    root3[...] = roots
+    gather_start(root3, root3_in, c_peers, 6)
 
     wait_bytes(pay2_in.at[pl.ds(0, NX - 1)], recv_sem.at[3])
     hi2, lo2 = split2(pay2_in[...].reshape(NX * 8, BLK))
@@ -294,10 +299,6 @@
             scale = inv[:, 128 * t : 128 * t + 1]
             nm[:, s] = nm[:, s] - pen[:, s] * (remote[q * ROWS : (q + 1) * ROWS] * scale)
 
-    wait_bytes(root2_in.at[pl.ds(0, NX * NY - 1)], recv_sem.at[5])
-    roots = jnp.sum(root2_in[...], axis=0)
-    root3[...] = roots
-    gather_start(root3, root3_in, c_peers, 6)
     wait_bytes(root3_in, recv_sem.at[6])
     roots = roots + root3_in[...]
     means = roots / roots[4:5]

time: 36.2 us -> 36.2 us (level)
  no operation moved by 1% of the time
where the time goes in v4:
time: 36.2 us; the launch traced here: 36.1 us
  Pallas kernels  33.9 us (94%)
  local copies, waits for them, and re-layouts  1.54 us (4%)
  between operations  0.64 us (2%)
    pallas_call x1, Pallas kernels, on_device(): pl.pallas_call(kernel, out_shape=(jax.ShapeDtypeStruct((ROWS, NV), F32),...  33.9 us
    unnamed x2, local copies, waits for them, and re-layouts  1.54 us

profile of v4, /device:TPU:1, one launch (start us, length us, event | category | flops | bytes accessed | tf_op | source)
XLA Modules:
  0.0 36.1 jit_solution(5027519072944587096)
XLA Ops:
  0.6 33.9 %shard_map.104 = (f32[64,2048]{1,0:T(8,128)S(1)}, f32[64,1536]{1,0:T(8,128)S(1)}) custom-call(bf16[2048,2048]{1,0:T(8,128)(2,1)} %k_h.1, f32[64,2048]{1,0:T(8,128)} %cost_h.1, f32[64,2048]{1,0:T(8,128)} %anchor_h.1, f32[64,2048]{1,0:T(8,128)} %cap_h.1, f32[64,1536]{1,0:T(8,128)} %mult_h.1, f32[1,2048]{1,0:T(1,128)} %bitcast.4, s32[1,64]{1,0:T(1,128)} %bitcast.5, ...), custom_call_target="tpu_custom_call" | custom-call | flops 4294967296 | bytes 12582912 | tf_op jit(solution)/shard_map/pallas_call | solution.py:322
  34.5 0.8 %copy.13 = f32[64,2048]{1,0:T(8,128)} copy(f32[64,2048]{1,0:T(8,128)S(1)} %get-tuple-element.4) | data formatting | bytes 1048576
  35.3 0.7 %copy.14 = f32[64,1536]{1,0:T(8,128)} copy(f32[64,1536]{1,0:T(8,128)S(1)} %get-tuple-element.5) | data formatting | bytes 786432

commit v5 on v4

--- a/solution.py
+++ b/solution.py
@@ -16,6 +16,7 @@
 NX, NY, NZ, NC = 4, 4, 8, 2
 F32 = jnp.float32
 BF16 = jnp.bfloat16
+GROUPS = {0: 4, 4: 7}
 XY_FAR_FIRST = (
     (2, 2), (2, 1), (2, 3), (1, 2), (3, 2), (2, 0), (0, 2), (1, 1), (1, 3), (3, 1), (3, 3),
     (1, 0), (3, 0), (0, 1), (0, 3),
@@ -98,7 +99,7 @@
                 barrier, inc=1, device_id=peer, device_id_type=pl.DeviceIdType.MESH
             )
 
-    greet(peers[:10])
+    greet(peers)
 
     def gather_start(src, dst, peers, index):
         for peer in peers:
@@ -117,7 +118,6 @@
     lin[:, 3 * SEC :] = cost[:, 3 * SEC :] - pen[:, 3 * SEC :] * anchor[:, 3 * SEC :]
     sc[...] = jnp.zeros((ROWS, NV), F32)
     rhs[0] = (start - lin[...]).astype(BF16)
-    greet(peers[10:])
 
     def block(j, cur, nxt, last):
         s = slice(j * BLK, (j + 1) * BLK)
@@ -132,14 +132,12 @@
         rhs[nxt, :, s] = ((new - rest) - lin[:, s]).astype(BF16)
         return new
 
-    def step(i):
-        for j in range(NBLK):
-            if i == 0 and j % 4 == 0:
-                for c in ks[j : j + 4]:
+    def step(i, first=0, end=NBLK):
+        for j in range(first, end):
+            if i == 0 and j in GROUPS:
+                for c in ks[j : GROUPS[j]]:
                     c.wait()
             block(j, i % 2, 1 - i % 2, False)
-
-    step(0)
 
     w_row = wv[...].astype(F32)
     ids = (n2v[...].astype(F32), n3v[...].astype(F32))
@@ -182,36 +180,13 @@
     meta1[...] = message
     meta1_in[z] = message
 
-    step(1)
-    step(2)
+    step(0, 0, NBLK - 1)
+    ks[NBLK - 1].wait()
     pl.semaphore_wait(barrier, len(peers))
     gather_start(meta1, meta1_in.at[z], z_peers, 0)
-    step(3)
-    step(4)
-    step(5)
-
-    wait_bytes(meta1_in.at[pl.ds(0, NZ - 1)], recv_sem.at[0])
-    line = jnp.sum(meta1_in[...], axis=0)
-    line_ids, line_w = line[0:1], line[1:2]
-    odd = row8 % 2 == 1
-    targ = jnp.sum(
-        jnp.where(lane == row8 + jnp.where(odd, 56, 0), line_ids, 0.0), axis=1, keepdims=True
-    )
-    before = jnp.sum(jnp.where(lane == row8 - 1, line_ids, 0.0), axis=1, keepdims=True)
-    group = (lane < 64) & ((lane % 8) // 2 == row8 // 2)
-    keep = jnp.logical_not(odd) | (targ != before)
-    spread = jnp.where(group & keep & (line_ids == targ), 1.0, 0.0)
-    line_weight = jnp.sum(spread * line_w, axis=1, keepdims=True)
-    place = lane == 64 + x * 8 + row8
-    put_ids = jnp.sum(jnp.where(place, targ, 0.0), axis=0, keepdims=True)
-    put_w = jnp.sum(jnp.where(place, line_weight, 0.0), axis=0, keepdims=True)
-    message = jnp.where(row8 == 0, put_ids, jnp.where(row8 == 1, put_w, 0.0))
-    meta2[...] = message
-    meta2_in[x] = message
-    coef_d[...] = (spread + pltpu.roll(spread, 64, 1)).astype(BF16)
-    gather_start(meta2, meta2_in.at[x], x_peers, 1)
-    step(6)
-
+    step(0, NBLK - 1)
+    for i in range(1, ITERS - 1):
+        step(i)
 
     def weighted(new, index):
         m = mask[index]
@@ -240,6 +215,28 @@
     gather_start(pay1, pay1_in.at[z], z_peers, 2)
     for j in range(6, NBLK):
         block(j, 1, 0, True)
+
+    wait_bytes(meta1_in.at[pl.ds(0, NZ - 1)], recv_sem.at[0])
+    line = jnp.sum(meta1_in[...], axis=0)
+    line_ids, line_w = line[0:1], line[1:2]
+    odd = row8 % 2 == 1
+    targ = jnp.sum(
+        jnp.where(lane == row8 + jnp.where(odd, 56, 0), line_ids, 0.0), axis=1, keepdims=True
+    )
+    before = jnp.sum(jnp.where(lane == row8 - 1, line_ids, 0.0), axis=1, keepdims=True)
+    group = (lane < 64) & ((lane % 8) // 2 == row8 // 2)
+    keep = jnp.logical_not(odd) | (targ != before)
+    spread = jnp.where(group & keep & (line_ids == targ), 1.0, 0.0)
+    line_weight = jnp.sum(spread * line_w, axis=1, keepdims=True)
+    place = lane == 64 + x * 8 + row8
+    put_ids = jnp.sum(jnp.where(place, targ, 0.0), axis=0, keepdims=True)
+    put_w = jnp.sum(jnp.where(place, line_weight, 0.0), axis=0, keepdims=True)
+    message = jnp.where(row8 == 0, put_ids, jnp.where(row8 == 1, put_w, 0.0))
+    meta2[...] = message
+    meta2_in[x] = message
+    coef_d[...] = (spread + pltpu.roll(spread, 64, 1)).astype(BF16)
+    gather_start(meta2, meta2_in.at[x], x_peers, 1)
+
 
     wait_bytes(root1_in.at[pl.ds(0, NZ - 1)], recv_sem.at[4])
     roots = jnp.sum(root1_in[...], axis=0)

time: 36.2 us -> 34.2 us (0.945)
  Pallas kernels: 33.9 us -> 32 us
    pallas_call x1, Pallas kernels: 33.9 us -> 32 us  [on_device(): pl.pallas_call(kernel, out_shape=(jax.ShapeDtypeStruct((ROWS, NV), F32),...]
where the time goes in v5:
time: 34.2 us
  Pallas kernels  32 us (94%)
  local copies, waits for them, and re-layouts  1.54 us (5%)
  between operations  0.64 us (2%)
    pallas_call x1, Pallas kernels, on_device(): pl.pallas_call(kernel, out_shape=(jax.ShapeDtypeStruct((ROWS, NV), F32),...  32 us
    unnamed x2, local copies, waits for them, and re-layouts  1.54 us

profile of v5, /device:TPU:1, one launch (start us, length us, event | category | flops | bytes accessed | tf_op | source)
XLA Modules:
  0.0 34.2 jit_solution(1609569874706107605)
XLA Ops:
  0.6 32.0 %shard_map.104 = (f32[64,2048]{1,0:T(8,128)S(1)}, f32[64,1536]{1,0:T(8,128)S(1)}) custom-call(bf16[2048,2048]{1,0:T(8,128)(2,1)} %k_h.1, f32[64,2048]{1,0:T(8,128)} %cost_h.1, f32[64,2048]{1,0:T(8,128)} %anchor_h.1, f32[64,2048]{1,0:T(8,128)} %cap_h.1, f32[64,1536]{1,0:T(8,128)} %mult_h.1, f32[1,2048]{1,0:T(1,128)} %bitcast.4, s32[1,64]{1,0:T(1,128)} %bitcast.5, ...), custom_call_target="tpu_custom_call" | custom-call | flops 4294967296 | bytes 12582912 | tf_op jit(solution)/shard_map/pallas_call | solution.py:319
  32.6 0.8 %copy.13 = f32[64,2048]{1,0:T(8,128)} copy(f32[64,2048]{1,0:T(8,128)S(1)} %get-tuple-element.4) | data formatting | bytes 1048576
  33.4 0.7 %copy.14 = f32[64,1536]{1,0:T(8,128)} copy(f32[64,1536]{1,0:T(8,128)S(1)} %get-tuple-element.5) | data formatting | bytes 786432
